TPU v7x, 32 devices: a whole 2x2x4 slice. The times are simulated.
32 devices in a mesh: section: 4 (over z), dp: 4 (over y, x), mp: 2 (over core).
Axes of the slice: x: 2, y: 2, z: 4, core: 2. Of those that a mesh axis runs over, the one named last changes fastest.
Arguments:
- held: bfloat16 [4, 4, 228, 12288], P('section', None, 'dp', 'mp'), may hold values from -6 to 6
- evict_map: int32 [4, 896, 1], P('section', 'dp'), may hold values from 0 to 3; in each aligned block of 224 rows (0 to 223, 224 to 447, ..., all dimensions but the last counted through in order) at most 57 rows name the same one
- cotangent: bfloat16 [4, 896, 12288], P('section', 'dp', 'mp'), may hold values from -6 to 6
- gain: float32 [4, 12288], P('section', 'mp'), may hold values from 0.25 to 1.75
Outputs:
- layer_input_gradient: bfloat16 [4, 896, 12288], P('section', 'dp', 'mp')
- grad_gain: float32 [4, 12288], P('section', 'mp')
Inputs may be any that keep to these rules, and one draw needn't show every extreme that they name: `evict_map`: in the tokens of one owner section and replica no holder is named by more than 57 tokens, a bound that some block reaches.
All inputs are finite; a program needn't handle non-finite values.
Results may differ from a plain program's by a relative error of at most 0.0004.
Values may be sent and summed in bfloat16 or wider, within the bound.
A program may use at most 64 MiB of HBM per device.

v0:
```python
import jax
import jax.numpy as jnp
from jax import lax
from jax.sharding import PartitionSpec as P

MODEL_WIDTH = 12288


def local(held, evict_map, cotangent, gain):
    sections = lax.axis_size("section")
    store = held[0]
    slot_count = store.shape[1]
    arrived = lax.all_to_all(store, "section", split_axis=0, concat_axis=0, tiled=True)
    holders = evict_map[0, :, 0]
    onehot = (holders[:, None] == jnp.arange(sections, dtype=jnp.int32)[None, :]).astype(jnp.int32)
    slots = jnp.sum(jnp.cumsum(onehot, axis=0) * onehot, axis=1) - 1
    flat = arrived.reshape(sections * slot_count, store.shape[2])
    saved_input = jnp.take(flat, holders * slot_count + slots, axis=0).astype(jnp.float32)
    first, second = lax.psum(
        (
            jnp.sum(saved_input, axis=1, keepdims=True),
            jnp.sum(saved_input * saved_input, axis=1, keepdims=True),
        ),
        "mp",
    )
    row_mean = first / MODEL_WIDTH
    inverse_deviation = 1.0 / jnp.sqrt(second / MODEL_WIDTH - row_mean * row_mean + 1e-05)
    normalized_input = (saved_input - row_mean) * inverse_deviation
    output_gradient = cotangent[0].astype(jnp.float32)
    gain_scaled_gradient = gain[0] * output_gradient
    sum_one, sum_two = lax.psum(
        (
            jnp.sum(gain_scaled_gradient, axis=1, keepdims=True),
            jnp.sum(gain_scaled_gradient * normalized_input, axis=1, keepdims=True),
        ),
        "mp",
    )
    first_gradient_mean = sum_one / MODEL_WIDTH
    second_gradient_mean = sum_two / MODEL_WIDTH
    layer_input_gradient = (
        inverse_deviation
        * (gain_scaled_gradient - first_gradient_mean - normalized_input * second_gradient_mean)
    ).astype(jnp.bfloat16)
    gain_product = jnp.sum(output_gradient * normalized_input, axis=0)
    grad_gain = lax.psum(gain_product, "dp")
    return (layer_input_gradient[None], grad_gain[None])


def solution(mesh):
    placed = (
        P("section", None, "dp", "mp"),
        P("section", "dp", None),
        P("section", "dp", "mp"),
        P("section", "mp"),
    )
    return jax.shard_map(
        local,
        mesh=mesh,
        in_specs=placed,
        out_specs=(P("section", "dp", "mp"), P("section", "mp")),
        check_vma=False,
    )
```

profile of v0, /device:TPU:0, one launch (start us, length us, event | category | flops | bytes accessed | tf_op | source)
XLA Modules:
  0.0 123.4 jit_solution(6136781789845492516)
XLA Ops:
  0.6 5.1 %copy.18 = bf16[1,4,57,6144]{3,2,1,0:T(8,128)(2,1)} copy(bf16[1,4,57,6144]{3,1,2,0:T(4,128)(2,1)} %param.4) | data formatting | bytes 5603328 | tf_op args[0]
  5.7 0.0 copy-start.2
  5.7 6.4 %all-to-all-start = ((bf16[4,57,6144]{2,1,0:T(8,128)(2,1)}), bf16[4,57,6144]{2,1,0:T(8,128)(2,1)}, u32[]{:S(2)}, u32[]{:S(2)}) async-start(bf16[4,57,6144]{2,1,0:T(8,128)(2,1)} %bitcast.44), calls=%async_computation | async-start | bytes 6291456 | tf_op jit(solution)/shard_map/all_to_all | solution.py:13
  12.1 0.0 copy-done.2
  12.2 1.2 reduce-window.6
  13.4 0.1 slice.14
  13.5 0.1 copy.12
  13.6 0.1 copy.13
  13.7 0.1 add_bitcast_fusion
  13.9 69.0 %all-to-all-done = bf16[4,57,6144]{2,1,0:T(8,128)(2,1)} async-done(((bf16[4,57,6144]{2,1,0:T(8,128)(2,1)}), bf16[4,57,6144]{2,1,0:T(8,128)(2,1)}, u32[]{:S(2)}, u32[]{:S(2)}) %all-to-all-start) | async-done | bytes 2801696 | tf_op jit(solution)/shard_map/all_to_all | solution.py:13
  82.9 2.8 %reshape.202 = bf16[228,6144]{1,0:T(8,128)(2,1)S(1)} reshape(bf16[4,57,6144]{2,1,0:T(8,128)(2,1)} %all-to-all-done) | data formatting | bytes 5603328 | tf_op jit(solution)/shard_map/reshape | solution.py:17
  85.7 0.0 copy-start.1
  85.7 3.7 %gather_fusion = bf16[224,6144]{1,0:T(8,128)(2,1)} fusion(bf16[228,6144]{1,0:T(8,128)(2,1)S(1)} %reshape.202, s32[1024]{0:T(1024)S(1)} %pad_clamp_fusion), kind=kCustom, calls=%fused_computation | custom fusion | bytes 5505920 | tf_op jit(solution)/shard_map/jit(_take)/gather | solution.py:18
  89.4 0.0 copy-start
  89.4 3.0 %convert_reduce_fusion = (f32[224]{0:T(256)S(1)}, f32[224]{0:T(256)S(1)}) fusion(bf16[224,6144]{1,0:T(8,128)(2,1)} %gather_fusion, pred[224]{0:T(512)(128)(4,1)S(1)} %compare_and_fusion), kind=kLoop, calls=%fused_computation.2 | loop fusion | flops 6880832 | bytes 2754528 | tf_op jit(solution)/shard_map/reduce_sum | solution.py:21
  92.4 2.5 %all-reduce.2 = (f32[224,1]{0,1:T(1,128)S(1)}, f32[224,1]{0,1:T(1,128)S(1)}) all-reduce(f32[224,1]{0,1:T(1,128)S(1)} %bitcast.61, f32[224,1]{0,1:T(1,128)S(1)} %bitcast.60), channel_id=1, replica_groups=mesh['section'=4,'dp'=4,'mp'=2] {'mp'}, use_global_device_ids=true, to_apply=%region_4.5 | all-reduce | flops 448 | bytes 3584 | tf_op jit(solution)/shard_map/psum | solution.py:19
  94.9 0.0 copy-done.1
  94.9 0.0 copy-done
  94.9 4.0 %fusion.5 = (f32[6144]{0:T(1024)S(1)}, f32[224]{0:T(256)S(1)}, f32[224]{0:T(256)S(1)}) fusion(bf16[1,224,6144]{2,1,0:T(8,128)(2,1)} %param.6, f32[224]{0:T(256)S(1)} %bitcast.56, f32[224]{0:T(256)S(1)} %bitcast.54, bf16[224,6144]{1,0:T(8,128)(2,1)S(1)} %copy-done, pred[224]{0:T(512)(128)(4,1)S(1)} %compare_and_fusion, f32[6144]{0:T(1024)S(1)} %bitcast.47), kind=kLoop, calls=%fused_computation.11 | loop fusion | flops 15132224 | bytes 5557984 | tf_op jit(solution)/shard_map/reduce_sum | solution.py:44
  98.9 16.9 %psum.39 = f32[1,6144]{1,0:T(1,128)} all-reduce(f32[1,6144]{1,0:T(1,128)S(1)} %bitcast.49), channel_id=1, replica_groups=mesh['section'=4,'dp'=4,'mp'=2] {'dp'}, use_global_device_ids=true, to_apply=%region_12.13 | all-reduce | flops 6144 | bytes 49152 | tf_op jit(solution)/shard_map/psum | solution.py:45
  115.8 2.4 %all-reduce.1 = (f32[224,1]{0,1:T(1,128)S(1)}, f32[224,1]{0,1:T(1,128)S(1)}) all-reduce(f32[224,1]{0,1:T(1,128)S(1)} %bitcast.58, f32[224,1]{0,1:T(1,128)S(1)} %bitcast.59), channel_id=1, replica_groups=mesh['section'=4,'dp'=4,'mp'=2] {'mp'}, use_global_device_ids=true, to_apply=%region_10.11 | all-reduce | flops 448 | bytes 3584 | tf_op jit(solution)/shard_map/psum | solution.py:31
  118.2 5.1 %fusion.9 = bf16[1,224,6144]{2,1,0:T(8,128)(2,1)} fusion(bf16[1,224,6144]{2,1,0:T(8,128)(2,1)} %param.6, bf16[224,6144]{1,0:T(8,128)(2,1)S(1)} %copy-done, f32[224]{0:T(256)S(1)} %bitcast.62, f32[224]{0:T(256)S(1)} %bitcast.55, f32[224]{0:T(256)S(1)} %bitcast.63, f32[6144]{0:T(1024)S(1)} %bitcast.48, f32[224]{0:T(256)S(1)} %bitcast.57, ...), kind=kLoop, calls=%fused_computation.15 | loop fusion | flops 15138816 | bytes 8285920 | tf_op jit(solution)/shard_map/convert_element_type | solution.py:43
  (13 shorter events, 0.1 us)
Async XLA Ops:
  5.7 6.5 %copy-start.2 = (s32[1,224,1]{1,2,0:T(1,128)S(1)}, s32[1,224,1]{1,2,0:T(1,128)}, u32[]{:S(2)}) copy-start(s32[1,224,1]{1,2,0:T(1,128)} %param.5) | copy-start | bytes 2692
  5.7 77.2 %all-to-all-start = ((bf16[4,57,6144]{2,1,0:T(8,128)(2,1)}), bf16[4,57,6144]{2,1,0:T(8,128)(2,1)}, u32[]{:S(2)}, u32[]{:S(2)}) async-start(bf16[4,57,6144]{2,1,0:T(8,128)(2,1)} %bitcast.44), calls=%async_computation | async-start | bytes 6291456 | tf_op jit(solution)/shard_map/all_to_all | solution.py:13
  85.7 9.2 %copy-start.1 = (f32[1,6144]{1,0:T(1,128)S(1)}, f32[1,6144]{1,0:T(1,128)}, u32[]{:S(2)}) copy-start(f32[1,6144]{1,0:T(1,128)} %param.7) | copy-start | bytes 73732
  89.4 5.5 %copy-start = (bf16[224,6144]{1,0:T(8,128)(2,1)S(1)}, bf16[224,6144]{1,0:T(8,128)(2,1)}, u32[]{:S(2)}) copy-start(bf16[224,6144]{1,0:T(8,128)(2,1)} %gather_fusion) | copy-start | bytes 8257540
where the time goes:
time: 124 us; the launch traced here: 123 us
  waiting for transfers between devices  69 us (56%)
  blocking collectives  21.8 us (18%)
  other arithmetic  13.5 us (11%)
  local copies, waits for them, and re-layouts  11.9 us (10%)
  starting transfers between devices  6.45 us (5%)
    all_to_all x1, waiting for transfers between devices, local(): lax.all_to_all(store, 'section', split_axis=0, concat_axis=0, tiled=True)  69 us
    psum x1, blocking collectives, local(): grad_gain = lax.psum(gain_product, 'dp')  16.9 us
    all_to_all x1, starting transfers between devices, local(): lax.all_to_all(store, 'section', split_axis=0, concat_axis=0, tiled=True)  6.45 us
    convert_element_type x1, other arithmetic, local(): layer_input_gradient = (inverse_deviation * (gain_scaled_gradient - first...  5.14 us
    unnamed x8, local copies, waits for them, and re-layouts  5.07 us
    reduce_sum x1, other arithmetic, local(): gain_product = jnp.sum(output_gradient * normalized_input, axis=0)  3.99 us
    gather x1, local copies, waits for them, and re-layouts, local(): jnp.take(flat, holders * slot_count + slots, axis=0).astype(jnp.float32)  3.74 us
    reduce_sum x1, other arithmetic, local(): jnp.sum(saved_input, axis=1, keepdims=True)  3 us
  transfers between devices with their start and end apart: 1, of which 1 were waited for; matrix products, arithmetic and copies ran while one was open for 1% of the time, Pallas kernels for 0%

commit v1 on v0

v1 whole, which is shorter than its diff:
```python
import functools

import jax
import jax.numpy as jnp
from jax import lax
from jax.experimental import pallas as pl
from jax.experimental.pallas import tpu as pltpu
from jax.sharding import PartitionSpec as P

MODEL_WIDTH = 12288
LANES = 128
BLOCK = 32
MESH = pl.DeviceIdType.MESH


def kernel(
    chunk, held, holders, cot_hbm, gain, dx_hbm, gg_out,
    recv, cot, xf, dx, place, part, stats, coef, gsum, gpart,
    send_sem, recv_sem, own_sem, cot_sem, mp_send, mp_recv, dp_send, dp_recv, out_sem,
):
    sections, slots, width = recv.shape
    rows = cot.shape[0]
    chunks = width // chunk
    blocks = rows // BLOCK
    tiles = chunk // LANES
    n_mp, n_dp = stats.shape[0], gpart.shape[0]
    me = lax.axis_index("section")
    my_mp = lax.axis_index("mp")
    my_dp = lax.axis_index("dp")

    barrier = pltpu.get_barrier_semaphore()
    for axis, mine, size in (("section", me, sections), ("mp", my_mp, n_mp), ("dp", my_dp, n_dp)):
        def greet(i, _, axis=axis, mine=mine, size=size):
            pl.semaphore_signal(
                barrier, inc=1, device_id={axis: lax.rem(mine + i, size)}, device_id_type=MESH
            )
            return 0
        lax.fori_loop(1, size, greet, 0)
    own_copy = pltpu.make_async_copy(held.at[0, me], recv.at[me], own_sem)
    cot_copy = pltpu.make_async_copy(cot_hbm.at[0], cot, cot_sem)
    pl.semaphore_wait(barrier, sections + n_mp + n_dp - 3)

    def columns(c):
        return pl.ds(pl.multiple_of(c * chunk, chunk), chunk)

    def outgoing(c, i):
        other = lax.rem(me + i, sections)
        return pltpu.make_async_remote_copy(
            src_ref=held.at[0, other, :, columns(c)],
            dst_ref=recv.at[me, :, columns(c)],
            send_sem=send_sem.at[c, i],
            recv_sem=recv_sem.at[c, me],
            device_id={"section": other},
            device_id_type=MESH,
        )

    def incoming(c, i):
        other = lax.rem(me + i, sections)
        return pltpu.make_async_remote_copy(
            src_ref=held.at[0, other, :, columns(c)],
            dst_ref=recv.at[other, :, columns(c)],
            send_sem=send_sem.at[c, i],
            recv_sem=recv_sem.at[c, other],
            device_id={"section": other},
            device_id_type=MESH,
        )

    def send(c, _):
        def one(i, _):
            outgoing(c, i).start()
            return 0
        return lax.fori_loop(1, sections, one, 0)
    lax.fori_loop(0, chunks, send, 0)
    own_copy.start()
    cot_copy.start()

    holder = holders[0]
    lane = lax.broadcasted_iota(jnp.int32, (rows, LANES), 1)
    onehot = jnp.where(holder == lane, 1.0, 0.0)
    upto = jnp.where(
        lax.broadcasted_iota(jnp.int32, (rows, rows), 0)
        >= lax.broadcasted_iota(jnp.int32, (rows, rows), 1),
        1.0, 0.0,
    ).astype(jnp.bfloat16)
    count = jnp.dot(upto, onehot.astype(jnp.bfloat16), preferred_element_type=jnp.float32)
    slot = jnp.sum(count * onehot, axis=1, keepdims=True) - 1.0
    key = holder.astype(jnp.float32) * slots + slot
    number = lax.broadcasted_iota(jnp.int32, (rows, slots), 1).astype(jnp.float32)
    for s in range(sections):
        place[s] = jnp.where(key == number + float(s * slots), 1.0, 0.0).astype(jnp.bfloat16)
    part[...] = jnp.zeros_like(part)
    gsum[...] = jnp.zeros_like(gsum)

    own_copy.wait()
    cot_copy.wait()

    def work(c, _):
        def arrive(i, _):
            incoming(c, i).wait_recv()
            return 0
        lax.fori_loop(1, sections, arrive, 0)
        cols = columns(c)
        total = jnp.dot(place[0], recv[0, :, cols], preferred_element_type=jnp.float32)
        for s in range(1, sections):
            total += jnp.dot(place[s], recv[s, :, cols], preferred_element_type=jnp.float32)
        xf[:, cols] = total

        def block(b, _):
            rws = pl.ds(pl.multiple_of(b * BLOCK, BLOCK), BLOCK)
            sums = [part[k, rws] for k in range(4)]
            for t in range(tiles):
                at = pl.ds(pl.multiple_of(c * chunk + t * LANES, LANES), LANES)
                x = xf[rws, at]
                g = gain[:, at] * cot[rws, at].astype(jnp.float32)
                sums = [sums[0] + x, sums[1] + x * x, sums[2] + g, sums[3] + g * x]
            for k in range(4):
                part[k, rws] = sums[k]
            return 0
        lax.fori_loop(0, blocks, block, 0)
        return 0
    lax.fori_loop(0, chunks, work, 0)

    lane = lax.broadcasted_iota(jnp.int32, (rows, LANES), 1)
    packed = jnp.zeros((rows, LANES), jnp.float32)
    for k in range(4):
        packed = jnp.where(lane == k, jnp.sum(part[k], axis=1, keepdims=True), packed)
    stats[my_mp] = packed

    def exchange(ref, axis, mine, size, sends, recvs, arriving):
        def copy(i):
            other = lax.rem(mine + i, size)
            return pltpu.make_async_remote_copy(
                src_ref=ref.at[mine],
                dst_ref=ref.at[other if arriving else mine],
                send_sem=sends.at[i],
                recv_sem=recvs.at[other if arriving else mine],
                device_id={axis: other},
                device_id_type=MESH,
            )
        return copy

    mp_out = exchange(stats, "mp", my_mp, n_mp, mp_send, mp_recv, False)
    mp_in = exchange(stats, "mp", my_mp, n_mp, mp_send, mp_recv, True)
    dp_out = exchange(gpart, "dp", my_dp, n_dp, dp_send, dp_recv, False)
    dp_in = exchange(gpart, "dp", my_dp, n_dp, dp_send, dp_recv, True)
    for i in range(1, n_mp):
        mp_out(i).start()
    for i in range(1, n_mp):
        mp_in(i).wait_recv()

    both = stats[0]
    for i in range(1, n_mp):
        both += stats[i]
    mean = both[:, 0:1] / MODEL_WIDTH
    rstd = 1.0 / jnp.sqrt(both[:, 1:2] / MODEL_WIDTH - mean * mean + 1e-05)
    m1 = both[:, 2:3] / MODEL_WIDTH
    m2 = rstd * (both[:, 3:4] / MODEL_WIDTH - mean * m1)
    for k, value in enumerate((mean, rstd, -rstd * rstd * m2, -rstd * m1)):
        coef[k] = jnp.broadcast_to(value, (rows, LANES))

    def gain_block(b, _):
        rws = pl.ds(pl.multiple_of(b * BLOCK, BLOCK), BLOCK)
        mean, rstd = coef[0, rws], coef[1, rws]

        def tile(t, _):
            at = pl.ds(pl.multiple_of(t * LANES, LANES), LANES)
            p = cot[rws, at].astype(jnp.float32) * ((xf[rws, at] - mean) * rstd)
            q = p[0:8]
            for j in range(8, BLOCK, 8):
                q += p[j:j + 8]
            gsum[:, at] += q
            return 0
        return lax.fori_loop(0, width // LANES, tile, 0, unroll=8)
    lax.fori_loop(0, blocks, gain_block, 0)
    gpart[my_dp] = jnp.sum(gsum[...], axis=0, keepdims=True)
    for i in range(1, n_dp):
        dp_out(i).start()

    def out_copy(b):
        rws = pl.ds(pl.multiple_of(b * BLOCK, BLOCK), BLOCK)
        return pltpu.make_async_copy(dx.at[rws], dx_hbm.at[0, rws], out_sem.at[b])

    def grad_block(b, _):
        rws = pl.ds(pl.multiple_of(b * BLOCK, BLOCK), BLOCK)
        mean, rstd, slope, shift = (coef[k, rws] for k in range(4))

        def tile(t, _):
            at = pl.ds(pl.multiple_of(t * LANES, LANES), LANES)
            g = gain[:, at] * cot[rws, at].astype(jnp.float32)
            dx[rws, at] = (rstd * g + shift + (xf[rws, at] - mean) * slope).astype(jnp.bfloat16)
            return 0
        lax.fori_loop(0, width // LANES, tile, 0, unroll=8)
        out_copy(b).start()
        return 0
    lax.fori_loop(0, blocks, grad_block, 0)

    for i in range(1, n_dp):
        dp_in(i).wait_recv()
    total = gpart[0]
    for i in range(1, n_dp):
        total += gpart[i]
    gg_out[...] = total

    def finish(b, _):
        out_copy(b).wait()
        return 0
    lax.fori_loop(0, blocks, finish, 0)
    for i in range(1, n_dp):
        dp_out(i).wait_send()
    for i in range(1, n_mp):
        mp_out(i).wait_send()

    def sent(c, _):
        def one(i, _):
            outgoing(c, i).wait_send()
            return 0
        return lax.fori_loop(1, sections, one, 0)
    lax.fori_loop(0, chunks, sent, 0)


def local(held, evict_map, cotangent, gain):
    sections, n_mp, n_dp = (lax.axis_size(a) for a in ("section", "mp", "dp"))
    _, _, slots, width = held.shape
    rows = cotangent.shape[1]
    chunk = 1024 if width % 1024 == 0 else width
    chunks = width // chunk
    anywhere = pl.BlockSpec(memory_space=pl.ANY)
    vmem = pl.BlockSpec(memory_space=pltpu.VMEM)
    dma = pltpu.SemaphoreType.DMA
    return pl.pallas_call(
        functools.partial(kernel, chunk),
        out_shape=(
            jax.ShapeDtypeStruct((1, rows, width), jnp.bfloat16),
            jax.ShapeDtypeStruct((1, width), jnp.float32),
        ),
        in_specs=[anywhere, vmem, anywhere, vmem],
        out_specs=(anywhere, vmem),
        scratch_shapes=[
            pltpu.VMEM((sections, slots, width), jnp.bfloat16),
            pltpu.VMEM((rows, width), jnp.bfloat16),
            pltpu.VMEM((rows, width), jnp.float32),
            pltpu.VMEM((rows, width), jnp.bfloat16),
            pltpu.VMEM((sections, rows, slots), jnp.bfloat16),
            pltpu.VMEM((4, rows, LANES), jnp.float32),
            pltpu.VMEM((n_mp, rows, LANES), jnp.float32),
            pltpu.VMEM((4, rows, LANES), jnp.float32),
            pltpu.VMEM((8, width), jnp.float32),
            pltpu.VMEM((n_dp, 1, width), jnp.float32),
            dma((chunks, sections)),
            dma((chunks, sections)),
            dma(()),
            dma(()),
            dma((n_mp,)),
            dma((n_mp,)),
            dma((n_dp,)),
            dma((n_dp,)),
            dma((rows // BLOCK,)),
        ],
        compiler_params=pltpu.CompilerParams(
            collective_id=0, has_side_effects=True, vmem_limit_bytes=48 * 1024 * 1024
        ),
        cost_estimate=pl.CostEstimate(
            flops=2 * rows * sections * slots * width,
            bytes_accessed=2 * width * (sections * slots + 2 * rows),
            transcendentals=0,
        ),
    )(held, evict_map, cotangent, gain)


def solution(mesh):
    placed = (
        P("section", None, "dp", "mp"),
        P("section", "dp", None),
        P("section", "dp", "mp"),
        P("section", "mp"),
    )
    return jax.shard_map(
        local,
        mesh=mesh,
        in_specs=placed,
        out_specs=(P("section", "dp", "mp"), P("section", "mp")),
        check_vma=False,
    )
```

time: 124 us -> 90.8 us (0.73)
  Pallas kernels: 0 us -> 81 us
  waiting for transfers between devices: 69 us -> 0 us
  blocking collectives: 21.8 us -> 0 us
  other arithmetic: 13.5 us -> 0 us
  starting transfers between devices: 6.45 us -> 0 us
  local copies, waits for them, and re-layouts: 11.9 us -> 8.11 us
    pallas_call x0 -> x1, Pallas kernels: none -> 81 us  [local(): pl.pallas_call(functools.partial(kernel, chunk), out_shape=(jax.ShapeDtyp...]
    all_to_all x1 -> x0, waiting for transfers between devices: 69 us -> none  [local(): lax.all_to_all(store, 'section', split_axis=0, concat_axis=0, tiled=True)]
    psum x3 -> x0, blocking collectives: 21.8 us -> none  [the longest x1 16.9 us: local(): grad_gain = lax.psum(gain_product, 'dp')]
    reduce_sum x3 -> x0, other arithmetic: 7.01 us -> none  [the longest x1 3.99 us: local(): gain_product = jnp.sum(output_gradient * normalized_input, axis=0)]
    all_to_all x1 -> x0, starting transfers between devices: 6.45 us -> none  [local(): lax.all_to_all(store, 'section', split_axis=0, concat_axis=0, tiled=True)]
    convert_element_type x1 -> x0, other arithmetic: 5.14 us -> none  [local(): layer_input_gradient = (inverse_deviation * (gain_scaled_gradient - first...]
    gather x1 -> x0, local copies, waits for them, and re-layouts: 3.74 us -> none  [local(): jnp.take(flat, holders * slot_count + slots, axis=0).astype(jnp.float32)]
    unnamed x8, local copies, waits for them, and re-layouts: 5.07 us -> 8.11 us
  transfers between devices with their start and end apart: 1 -> 0, of which waited for: 1 -> 0; matrix products, arithmetic and copies ran while one was open for 1% -> 0% of each run, Pallas kernels for 0% -> 0%
where the time goes in v1:
time: 90.8 us; the launch traced here: 89.7 us
  Pallas kernels  81 us (89%)
  local copies, waits for them, and re-layouts  8.11 us (9%)
    pallas_call x1, Pallas kernels, local(): pl.pallas_call(functools.partial(kernel, chunk), out_shape=(jax.ShapeDtyp...  81 us
    unnamed x8, local copies, waits for them, and re-layouts  8.11 us

profile of v1, /device:TPU:0, one launch (start us, length us, event | category | flops | bytes accessed | tf_op | source)
XLA Modules:
  0.0 89.7 jit_solution(13685626825075479272)
XLA Ops:
  0.6 0.8 copy.7.holders
  1.4 0.0 copy-start
  1.4 0.0 copy-start.1
  1.5 5.2 %copy.6.held = bf16[1,4,57,6144]{3,2,1,0:T(8,128)(2,1)} copy(bf16[1,4,57,6144]{3,1,2,0:T(4,128)(2,1)} %param.4) | data formatting | bytes 5603328 | tf_op args[0]
  6.6 0.0 copy-done
  6.6 0.0 copy-done.1
  6.6 81.0 %shard_map.59 = (bf16[1,224,6144]{2,1,0:T(8,128)(2,1)S(1)}, f32[1,6144]{1,0:T(1,128)S(1)}) custom-call(bf16[1,4,57,6144]{3,2,1,0:T(8,128)(2,1)} %copy.6.held, s32[1,224,1]{2,1,0:T(8,128)S(1)} %copy.7.holders, bf16[1,224,6144]{2,1,0:T(8,128)(2,1)S(1)} %copy-done, f32[1,6144]{1,0:T(1,128)S(1)} %copy-done.1), custom_call_target="tpu_custom_call" | custom-call | flops 627572736 | bytes 8306688 | tf_op jit(solution)/shard_map/pallas_call | solution.py:230
  87.6 1.5 %copy.10 = bf16[1,224,6144]{2,1,0:T(8,128)(2,1)} copy(bf16[1,224,6144]{2,1,0:T(8,128)(2,1)S(1)} %get-tuple-element.4) | data formatting | bytes 5505024
  89.1 0.6 copy.11
Async XLA Ops:
  1.4 5.2 %copy-start = (bf16[1,224,6144]{2,1,0:T(8,128)(2,1)S(1)}, bf16[1,224,6144]{2,1,0:T(8,128)(2,1)}, u32[]{:S(2)}) copy-start(bf16[1,224,6144]{2,1,0:T(8,128)(2,1)} %cot_hbm.1) | copy-start | bytes 8257540
  1.4 5.2 %copy-start.1 = (f32[1,6144]{1,0:T(1,128)S(1)}, f32[1,6144]{1,0:T(1,128)}, u32[]{:S(2)}) copy-start(f32[1,6144]{1,0:T(1,128)} %gain.1) | copy-start | bytes 73732

commit v2 on v1

--- a/solution.py
+++ b/solution.py
@@ -14,11 +14,15 @@
 
 
 def kernel(
-    chunk, held, holders, cot_hbm, gain, dx_hbm, gg_out,
-    recv, cot, xf, dx, place, part, stats, coef, gsum, gpart,
-    send_sem, recv_sem, own_sem, cot_sem, mp_send, mp_recv, dp_send, dp_recv, out_sem,
+    chunk, held, holders_hbm, cot_hbm, gain_hbm, dx_hbm, gg_out,
+    mixed, outbox, recv, odd_out, odd_in, holders, gain, cot, xf, dx, place, part, stats, coef, gsum, gpart,
+    held_sem, send_sem, recv_sem, odd_held_sem, odd_send, odd_recv, holders_sem, gain_sem, cot_sem,
+    mp_send, mp_recv, dp_send, dp_recv, out_sem,
 ):
-    sections, slots, width = recv.shape
+    slots, sections, width = held.shape
+    padded = recv.shape[1]
+    main = min(slots, padded)
+    odd = slots - main
     rows = cot.shape[0]
     chunks = width // chunk
     blocks = rows // BLOCK
@@ -36,17 +40,40 @@
             )
             return 0
         lax.fori_loop(1, size, greet, 0)
-    own_copy = pltpu.make_async_copy(held.at[0, me], recv.at[me], own_sem)
-    cot_copy = pltpu.make_async_copy(cot_hbm.at[0], cot, cot_sem)
-    pl.semaphore_wait(barrier, sections + n_mp + n_dp - 3)
 
     def columns(c):
         return pl.ds(pl.multiple_of(c * chunk, chunk), chunk)
+
+    def fetch(c):
+        return pltpu.make_async_copy(
+            held.at[0:main, :, columns(c)], mixed.at[0:main, :, columns(c)], held_sem.at[c]
+        )
+    def start_fetch(c, _):
+        fetch(c).start()
+        return 0
+    lax.fori_loop(0, chunks, start_fetch, 0)
+    if odd:
+        odd_fetch = pltpu.make_async_copy(
+            held.at[main:slots], mixed.at[main:slots], odd_held_sem
+        )
+        odd_fetch.start()
+    cot_copy = pltpu.make_async_copy(cot_hbm.at[0], cot, cot_sem)
+    cot_copy.start()
+    holders_copy = pltpu.make_async_copy(holders_hbm, holders, holders_sem)
+    holders_copy.start()
+    gain_copy = pltpu.make_async_copy(gain_hbm, gain, gain_sem)
+    gain_copy.start()
+
+    here = lax.broadcasted_iota(jnp.int32, (padded, main * sections), 0)
+    there = lax.broadcasted_iota(jnp.int32, (padded, main * sections), 1)
+    by_owner = jnp.concatenate(
+        [jnp.where(here * sections + s == there, 1.0, 0.0) for s in range(sections)], axis=0
+    ).astype(jnp.bfloat16)
 
     def outgoing(c, i):
         other = lax.rem(me + i, sections)
         return pltpu.make_async_remote_copy(
-            src_ref=held.at[0, other, :, columns(c)],
+            src_ref=outbox.at[other, :, columns(c)],
             dst_ref=recv.at[me, :, columns(c)],
             send_sem=send_sem.at[c, i],
             recv_sem=recv_sem.at[c, me],
@@ -57,7 +84,7 @@
     def incoming(c, i):
         other = lax.rem(me + i, sections)
         return pltpu.make_async_remote_copy(
-            src_ref=held.at[0, other, :, columns(c)],
+            src_ref=outbox.at[other, :, columns(c)],
             dst_ref=recv.at[other, :, columns(c)],
             send_sem=send_sem.at[c, i],
             recv_sem=recv_sem.at[c, other],
@@ -65,34 +92,83 @@
             device_id_type=MESH,
         )
 
+    def odd_copy(i, arriving):
+        other = lax.rem(me + i, sections)
+        origin = other if arriving else me
+        return pltpu.make_async_remote_copy(
+            src_ref=odd_out.at[other],
+            dst_ref=odd_in.at[origin],
+            send_sem=odd_send.at[i],
+            recv_sem=odd_recv.at[origin],
+            device_id={"section": other},
+            device_id_type=MESH,
+        )
+
     def send(c, _):
+        fetch(c).wait()
+        cols = columns(c)
+        rows_by_slot = mixed[0:main, :, cols].reshape(main * sections, chunk)
+        sorted_rows = jnp.dot(
+            by_owner, rows_by_slot, preferred_element_type=jnp.float32
+        ).astype(jnp.bfloat16)
+        for s in range(sections):
+            outbox[s, :, cols] = sorted_rows[s * padded:(s + 1) * padded]
+
         def one(i, _):
             outgoing(c, i).start()
             return 0
-        return lax.fori_loop(1, sections, one, 0)
-    lax.fori_loop(0, chunks, send, 0)
-    own_copy.start()
-    cot_copy.start()
-
-    holder = holders[0]
+        lax.fori_loop(1, sections, one, 0)
+        recv[me, :, cols] = outbox[me, :, cols]
+        return 0
+
+    pl.semaphore_wait(barrier, sections + n_mp + n_dp - 3)
+    send(0, 0)
+    if odd:
+        odd_fetch.wait()
+        for k in range(odd):
+            last = mixed[main + k].astype(jnp.float32)
+            for s in range(sections):
+                odd_out[s, k:k + 1, :] = last[s:s + 1]
+
+        def send_odd(i, _):
+            odd_copy(i, False).start()
+            return 0
+        lax.fori_loop(1, sections, send_odd, 0)
+        odd_in[me] = odd_out[me]
+    lax.fori_loop(1, chunks, send, 0)
+
+    holders_copy.wait()
+    across = lax.broadcasted_iota(jnp.int32, (rows, rows), 1)
+    down = lax.broadcasted_iota(jnp.int32, (rows, rows), 0)
+    named = holders[...].astype(jnp.float32)
+    holder = jnp.sum(jnp.where(across == down, named, 0.0), axis=1, keepdims=True)
     lane = lax.broadcasted_iota(jnp.int32, (rows, LANES), 1)
-    onehot = jnp.where(holder == lane, 1.0, 0.0)
-    upto = jnp.where(
-        lax.broadcasted_iota(jnp.int32, (rows, rows), 0)
-        >= lax.broadcasted_iota(jnp.int32, (rows, rows), 1),
-        1.0, 0.0,
-    ).astype(jnp.bfloat16)
+    onehot = jnp.where(holder == lane.astype(jnp.float32), 1.0, 0.0)
+    upto = jnp.where(down >= across, 1.0, 0.0).astype(jnp.bfloat16)
     count = jnp.dot(upto, onehot.astype(jnp.bfloat16), preferred_element_type=jnp.float32)
     slot = jnp.sum(count * onehot, axis=1, keepdims=True) - 1.0
-    key = holder.astype(jnp.float32) * slots + slot
-    number = lax.broadcasted_iota(jnp.int32, (rows, slots), 1).astype(jnp.float32)
+    number = lax.broadcasted_iota(jnp.int32, (rows, padded), 1).astype(jnp.float32)
     for s in range(sections):
-        place[s] = jnp.where(key == number + float(s * slots), 1.0, 0.0).astype(jnp.bfloat16)
+        place[s] = jnp.where(
+            jnp.logical_and(holder == float(s), slot == number), 1.0, 0.0
+        ).astype(jnp.bfloat16)
+    number = lax.broadcasted_iota(jnp.int32, (rows, sections), 1).astype(jnp.float32)
+    odd_place = [
+        jnp.where(
+            jnp.logical_and(holder == number, slot == float(main + k)), 1.0, 0.0
+        ).astype(jnp.bfloat16)
+        for k in range(odd)
+    ]
     part[...] = jnp.zeros_like(part)
     gsum[...] = jnp.zeros_like(gsum)
 
-    own_copy.wait()
     cot_copy.wait()
+    gain_copy.wait()
+    if odd:
+        def odd_arrive(i, _):
+            odd_copy(i, True).wait_recv()
+            return 0
+        lax.fori_loop(1, sections, odd_arrive, 0)
 
     def work(c, _):
         def arrive(i, _):
@@ -103,6 +179,11 @@
         total = jnp.dot(place[0], recv[0, :, cols], preferred_element_type=jnp.float32)
         for s in range(1, sections):
             total += jnp.dot(place[s], recv[s, :, cols], preferred_element_type=jnp.float32)
+        for k in range(odd):
+            extra = jnp.concatenate([odd_in[s, k:k + 1, cols] for s in range(sections)], axis=0)
+            total += jnp.dot(
+                odd_place[k], extra.astype(jnp.bfloat16), preferred_element_type=jnp.float32
+            )
         xf[:, cols] = total
 
         def block(b, _):
@@ -205,6 +286,7 @@
         out_copy(b).wait()
         return 0
     lax.fori_loop(0, blocks, finish, 0)
+
     for i in range(1, n_dp):
         dp_out(i).wait_send()
     for i in range(1, n_mp):
@@ -216,15 +298,22 @@
             return 0
         return lax.fori_loop(1, sections, one, 0)
     lax.fori_loop(0, chunks, sent, 0)
+    if odd:
+        def odd_sent(i, _):
+            odd_copy(i, False).wait_send()
+            return 0
+        lax.fori_loop(1, sections, odd_sent, 0)
 
 
 def local(held, evict_map, cotangent, gain):
     sections, n_mp, n_dp = (lax.axis_size(a) for a in ("section", "mp", "dp"))
     _, _, slots, width = held.shape
     rows = cotangent.shape[1]
-    chunk = 1024 if width % 1024 == 0 else width
+    chunk = 512 if width % 512 == 0 else width
     chunks = width // chunk
-    anywhere = pl.BlockSpec(memory_space=pl.ANY)
+    odd = slots % 8 if slots > 8 and slots % 8 <= 3 else 0
+    padded = -(-(slots - odd) // 8) * 8
+    outside = pl.BlockSpec(memory_space=pltpu.HBM)
     vmem = pl.BlockSpec(memory_space=pltpu.VMEM)
     dma = pltpu.SemaphoreType.DMA
     return pl.pallas_call(
@@ -233,21 +322,32 @@
             jax.ShapeDtypeStruct((1, rows, width), jnp.bfloat16),
             jax.ShapeDtypeStruct((1, width), jnp.float32),
         ),
-        in_specs=[anywhere, vmem, anywhere, vmem],
-        out_specs=(anywhere, vmem),
+        in_specs=[outside] * 4,
+        out_specs=(outside, vmem),
         scratch_shapes=[
-            pltpu.VMEM((sections, slots, width), jnp.bfloat16),
+            pltpu.VMEM((slots, sections, width), jnp.bfloat16),
+            pltpu.VMEM((sections, padded, width), jnp.bfloat16),
+            pltpu.VMEM((sections, padded, width), jnp.bfloat16),
+            pltpu.VMEM((sections, max(odd, 1), width), jnp.float32),
+            pltpu.VMEM((sections, max(odd, 1), width), jnp.float32),
+            pltpu.VMEM((1, rows), jnp.int32),
+            pltpu.VMEM((1, width), jnp.float32),
             pltpu.VMEM((rows, width), jnp.bfloat16),
             pltpu.VMEM((rows, width), jnp.float32),
             pltpu.VMEM((rows, width), jnp.bfloat16),
-            pltpu.VMEM((sections, rows, slots), jnp.bfloat16),
+            pltpu.VMEM((sections, rows, padded), jnp.bfloat16),
             pltpu.VMEM((4, rows, LANES), jnp.float32),
             pltpu.VMEM((n_mp, rows, LANES), jnp.float32),
             pltpu.VMEM((4, rows, LANES), jnp.float32),
             pltpu.VMEM((8, width), jnp.float32),
             pltpu.VMEM((n_dp, 1, width), jnp.float32),
+            dma((chunks,)),
             dma((chunks, sections)),
             dma((chunks, sections)),
+            dma(()),
+            dma((sections,)),
+            dma((sections,)),
+            dma(()),
             dma(()),
             dma(()),
             dma((n_mp,)),
@@ -257,14 +357,14 @@
             dma((rows // BLOCK,)),
         ],
         compiler_params=pltpu.CompilerParams(
-            collective_id=0, has_side_effects=True, vmem_limit_bytes=48 * 1024 * 1024
+            collective_id=0, has_side_effects=True, vmem_limit_bytes=56 * 1024 * 1024
         ),
         cost_estimate=pl.CostEstimate(
             flops=2 * rows * sections * slots * width,
             bytes_accessed=2 * width * (sections * slots + 2 * rows),
             transcendentals=0,
         ),
-    )(held, evict_map, cotangent, gain)
+    )(jnp.transpose(held[0], (1, 0, 2)), evict_map.reshape(1, rows), cotangent, gain)
 
 
 def solution(mesh):

time: 90.8 us -> 82.1 us (0.904)
  Pallas kernels: 81 us -> 76.6 us
  local copies, waits for them, and re-layouts: 8.11 us -> 4.22 us
    pallas_call x1, Pallas kernels: 81 us -> 76.6 us  [local(): pl.pallas_call(functools.partial(kernel, chunk), out_shape=(jax.ShapeDtyp...]
    unnamed x8 -> x4, local copies, waits for them, and re-layouts: 8.11 us -> 4.22 us
where the time goes in v2:
time: 82.1 us; the launch traced here: 81.5 us
  Pallas kernels  76.6 us (93%)
  local copies, waits for them, and re-layouts  4.22 us (5%)
    pallas_call x1, Pallas kernels, local(): pl.pallas_call(functools.partial(kernel, chunk), out_shape=(jax.ShapeDtyp...  76.6 us
    unnamed x4, local copies, waits for them, and re-layouts  4.22 us

profile of v2, /device:TPU:0, one launch (start us, length us, event | category | flops | bytes accessed | tf_op | source)
XLA Modules:
  0.0 81.5 jit_solution(7581055615218548755)
XLA Ops:
  0.6 76.6 %shard_map.59 = (bf16[1,224,6144]{2,1,0:T(8,128)(2,1)}, f32[1,6144]{1,0:T(1,128)}) custom-call(bf16[57,4,6144]{2,1,0:T(4,128)(2,1)} %bitcast.4, s32[1,224]{1,0:T(1,128)} %bitcast.5, bf16[1,224,6144]{2,1,0:T(8,128)(2,1)} %cot_hbm.1, f32[1,6144]{1,0:T(1,128)} %gain_hbm.1), custom_call_target="tpu_custom_call" | custom-call | flops 627572736 | bytes 8306688 | tf_op jit(solution)/shard_map/pallas_call | solution.py:319
  77.3 0.0 copy-start
  77.3 3.6 %copy.8 = bf16[1,224,6144]{2,1,0:T(8,128)(2,1)} copy(bf16[1,224,6144]{2,1,0:T(8,128)(2,1)} %get-tuple-element.4) | data formatting | bytes 5505024
  80.9 0.0 copy-done
  80.9 0.6 copy.9
Async XLA Ops:
  77.3 3.6 %copy-start = (f32[1,6144]{1,0:T(1,128)S(1)}, f32[1,6144]{1,0:T(1,128)}, u32[]{:S(2)}) copy-start(f32[1,6144]{1,0:T(1,128)} %get-tuple-element.5) | copy-start | bytes 73732

commit v3 on v2

--- a/solution.py
+++ b/solution.py
@@ -14,10 +14,10 @@
 
 
 def kernel(
-    chunk, held, holders_hbm, cot_hbm, gain_hbm, dx_hbm, gg_out,
-    mixed, outbox, recv, odd_out, odd_in, holders, gain, cot, xf, dx, place, part, stats, coef, gsum, gpart,
+    chunk, held, holders_hbm, cot_hbm, gain_hbm, dx, gg_out,
+    mixed, outbox, recv, odd_out, odd_in, holders, gain, cot, xf, place, part, stats, coef, gsum, gpart,
     held_sem, send_sem, recv_sem, odd_held_sem, odd_send, odd_recv, holders_sem, gain_sem, cot_sem,
-    mp_send, mp_recv, dp_send, dp_recv, out_sem,
+    mp_send, mp_recv, dp_send, dp_recv,
 ):
     slots, sections, width = held.shape
     padded = recv.shape[1]
@@ -257,10 +257,6 @@
     for i in range(1, n_dp):
         dp_out(i).start()
 
-    def out_copy(b):
-        rws = pl.ds(pl.multiple_of(b * BLOCK, BLOCK), BLOCK)
-        return pltpu.make_async_copy(dx.at[rws], dx_hbm.at[0, rws], out_sem.at[b])
-
     def grad_block(b, _):
         rws = pl.ds(pl.multiple_of(b * BLOCK, BLOCK), BLOCK)
         mean, rstd, slope, shift = (coef[k, rws] for k in range(4))
@@ -268,10 +264,9 @@
         def tile(t, _):
             at = pl.ds(pl.multiple_of(t * LANES, LANES), LANES)
             g = gain[:, at] * cot[rws, at].astype(jnp.float32)
-            dx[rws, at] = (rstd * g + shift + (xf[rws, at] - mean) * slope).astype(jnp.bfloat16)
+            dx[0, rws, at] = (rstd * g + shift + (xf[rws, at] - mean) * slope).astype(jnp.bfloat16)
             return 0
         lax.fori_loop(0, width // LANES, tile, 0, unroll=8)
-        out_copy(b).start()
         return 0
     lax.fori_loop(0, blocks, grad_block, 0)
 
@@ -281,11 +276,6 @@
     for i in range(1, n_dp):
         total += gpart[i]
     gg_out[...] = total
-
-    def finish(b, _):
-        out_copy(b).wait()
-        return 0
-    lax.fori_loop(0, blocks, finish, 0)
 
     for i in range(1, n_dp):
         dp_out(i).wait_send()
@@ -319,11 +309,11 @@
     return pl.pallas_call(
         functools.partial(kernel, chunk),
         out_shape=(
-            jax.ShapeDtypeStruct((1, rows, width), jnp.bfloat16),
-            jax.ShapeDtypeStruct((1, width), jnp.float32),
+            pltpu.VMEM((1, rows, width), jnp.bfloat16),
+            pltpu.VMEM((1, width), jnp.float32),
         ),
         in_specs=[outside] * 4,
-        out_specs=(outside, vmem),
+        out_specs=(vmem, vmem),
         scratch_shapes=[
             pltpu.VMEM((slots, sections, width), jnp.bfloat16),
             pltpu.VMEM((sections, padded, width), jnp.bfloat16),
@@ -334,7 +324,6 @@
             pltpu.VMEM((1, width), jnp.float32),
             pltpu.VMEM((rows, width), jnp.bfloat16),
             pltpu.VMEM((rows, width), jnp.float32),
-            pltpu.VMEM((rows, width), jnp.bfloat16),
             pltpu.VMEM((sections, rows, padded), jnp.bfloat16),
             pltpu.VMEM((4, rows, LANES), jnp.float32),
             pltpu.VMEM((n_mp, rows, LANES), jnp.float32),
@@ -354,7 +343,6 @@
             dma((n_mp,)),
             dma((n_dp,)),
             dma((n_dp,)),
-            dma((rows // BLOCK,)),
         ],
         compiler_params=pltpu.CompilerParams(
             collective_id=0, has_side_effects=True, vmem_limit_bytes=56 * 1024 * 1024

time: 82.1 us -> 78.8 us (0.960)
  local copies, waits for them, and re-layouts: 4.22 us -> 2.14 us
    unnamed x4 -> x2, local copies, waits for them, and re-layouts: 4.22 us -> 2.14 us
where the time goes in v3:
time: 78.8 us; the launch traced here: 78.7 us
  Pallas kernels  75.9 us (96%)
  local copies, waits for them, and re-layouts  2.14 us (3%)
    pallas_call x1, Pallas kernels, local(): pl.pallas_call(functools.partial(kernel, chunk), out_shape=(pltpu.VMEM((1...  75.9 us
    unnamed x2, local copies, waits for them, and re-layouts  2.14 us

profile of v3, /device:TPU:0, one launch (start us, length us, event | category | flops | bytes accessed | tf_op | source)
XLA Modules:
  0.0 78.7 jit_solution(18293857371949288687)
XLA Ops:
  0.6 75.9 %shard_map.59 = (bf16[1,224,6144]{2,1,0:T(8,128)(2,1)S(1)}, f32[1,6144]{1,0:T(1,128)S(1)}) custom-call(bf16[57,4,6144]{2,1,0:T(4,128)(2,1)} %bitcast.4, s32[1,224]{1,0:T(1,128)} %bitcast.5, bf16[1,224,6144]{2,1,0:T(8,128)(2,1)} %cot_hbm.1, f32[1,6144]{1,0:T(1,128)} %gain_hbm.1), custom_call_target="tpu_custom_call" | custom-call | flops 627572736 | bytes 8306688 | tf_op jit(solution)/shard_map/pallas_call | solution.py:309
  76.5 1.5 %copy.8 = bf16[1,224,6144]{2,1,0:T(8,128)(2,1)} copy(bf16[1,224,6144]{2,1,0:T(8,128)(2,1)S(1)} %get-tuple-element.2) | data formatting | bytes 5505024
  78.1 0.6 copy.9

commit v4 on v3

--- a/solution.py
+++ b/solution.py
@@ -115,7 +115,7 @@
             outbox[s, :, cols] = sorted_rows[s * padded:(s + 1) * padded]
 
         def one(i, _):
-            outgoing(c, i).start()
+            outgoing(c, jnp.where(2 * me < sections, sections - i, i)).start()
             return 0
         lax.fori_loop(1, sections, one, 0)
         recv[me, :, cols] = outbox[me, :, cols]

time: 78.8 us -> 78.9 us (level)
  no operation moved by 1% of the time
where the time goes in v4:
time: 78.9 us; the launch traced here: 78.7 us
  Pallas kernels  75.9 us (96%)
  local copies, waits for them, and re-layouts  2.14 us (3%)
    pallas_call x1, Pallas kernels, local(): pl.pallas_call(functools.partial(kernel, chunk), out_shape=(pltpu.VMEM((1...  75.9 us
    unnamed x2, local copies, waits for them, and re-layouts  2.14 us

profile of v4, /device:TPU:0, one launch (start us, length us, event | category | flops | bytes accessed | tf_op | source)
XLA Modules:
  0.0 78.7 jit_solution(17062385198583041458)
XLA Ops:
  0.6 75.9 %shard_map.59 = (bf16[1,224,6144]{2,1,0:T(8,128)(2,1)S(1)}, f32[1,6144]{1,0:T(1,128)S(1)}) custom-call(bf16[57,4,6144]{2,1,0:T(4,128)(2,1)} %bitcast.4, s32[1,224]{1,0:T(1,128)} %bitcast.5, bf16[1,224,6144]{2,1,0:T(8,128)(2,1)} %cot_hbm.1, f32[1,6144]{1,0:T(1,128)} %gain_hbm.1), custom_call_target="tpu_custom_call" | custom-call | flops 627572736 | bytes 8306688 | tf_op jit(solution)/shard_map/pallas_call | solution.py:309
  76.6 1.5 %copy.8 = bf16[1,224,6144]{2,1,0:T(8,128)(2,1)} copy(bf16[1,224,6144]{2,1,0:T(8,128)(2,1)S(1)} %get-tuple-element.2) | data formatting | bytes 5505024
  78.1 0.6 copy.9

commit v5 on v4

--- a/solution.py
+++ b/solution.py
@@ -299,7 +299,7 @@
     sections, n_mp, n_dp = (lax.axis_size(a) for a in ("section", "mp", "dp"))
     _, _, slots, width = held.shape
     rows = cotangent.shape[1]
-    chunk = 512 if width % 512 == 0 else width
+    chunk = 1024 if width % 1024 == 0 else width
     chunks = width // chunk
     odd = slots % 8 if slots > 8 and slots % 8 <= 3 else 0
     padded = -(-(slots - odd) // 8) * 8

time: 78.9 us -> 77.9 us (0.987)
  Pallas kernels: 75.9 us -> 75 us
    pallas_call x1, Pallas kernels: 75.9 us -> 75 us  [local(): pl.pallas_call(functools.partial(kernel, chunk), out_shape=(pltpu.VMEM((1...]
where the time goes in v5:
time: 77.9 us; the launch traced here: 77.8 us
  Pallas kernels  75 us (96%)
  local copies, waits for them, and re-layouts  2.14 us (3%)
    pallas_call x1, Pallas kernels, local(): pl.pallas_call(functools.partial(kernel, chunk), out_shape=(pltpu.VMEM((1...  75 us
    unnamed x2, local copies, waits for them, and re-layouts  2.14 us

profile of v5, /device:TPU:0, one launch (start us, length us, event | category | flops | bytes accessed | tf_op | source)
XLA Modules:
  0.0 77.8 jit_solution(4781885521170891934)
XLA Ops:
  0.6 75.0 %shard_map.59 = (bf16[1,224,6144]{2,1,0:T(8,128)(2,1)S(1)}, f32[1,6144]{1,0:T(1,128)S(1)}) custom-call(bf16[57,4,6144]{2,1,0:T(4,128)(2,1)} %bitcast.4, s32[1,224]{1,0:T(1,128)} %bitcast.5, bf16[1,224,6144]{2,1,0:T(8,128)(2,1)} %cot_hbm.1, f32[1,6144]{1,0:T(1,128)} %gain_hbm.1), custom_call_target="tpu_custom_call" | custom-call | flops 627572736 | bytes 8306688 | tf_op jit(solution)/shard_map/pallas_call | solution.py:309
  75.6 1.5 %copy.8 = bf16[1,224,6144]{2,1,0:T(8,128)(2,1)} copy(bf16[1,224,6144]{2,1,0:T(8,128)(2,1)S(1)} %get-tuple-element.2) | data formatting | bytes 5505024
  77.2 0.6 copy.9
